TPU v7x, 32 devices: a whole 2x2x4 slice. The times are simulated.
32 devices in a mesh: dp: 16 (over z, y, core), mp: 2 (over x).
Axes of the slice: x: 2, y: 2, z: 4, core: 2. Of those that a mesh axis runs over, the one named last changes fastest.
Arguments:
- layer_input: bfloat16 [24576, 768], P('dp'), may hold values from -9 to 9
- page_boxes: int32 [24576, 4], P('dp'), may hold values from 0 to 1000
- output_grad: bfloat16 [24576, 768], P('dp'), may hold values from -6 to 6
- attn_proj: float32 [3, 768, 768], P(None, 'dp', 'mp'), may hold values from -0.21875 to 0.21875
- attn_first: float32 [3, 768, 768], P(None, 'dp', 'mp'), may hold values from -2.670288e-05 to 2.670288e-05
- attn_second: float32 [3, 768, 768], P(None, 'dp', 'mp'), may hold values from 6.958547e-13 to 1.1133676e-11
- box_proj: float32 [128, 768], P('dp', 'mp'), may hold values from -0.75 to 0.75
- box_first: float32 [128, 768], P('dp', 'mp'), may hold values from -2.670288e-05 to 2.670288e-05
- box_second: float32 [128, 768], P('dp', 'mp'), may hold values from 6.958547e-13 to 1.1133676e-11
- merge_proj: float32 [768, 768], P('mp', 'dp'), may hold values from -1.25 to 1.25
- merge_first: float32 [768, 768], P('mp', 'dp'), may hold values from -2.670288e-05 to 2.670288e-05
- merge_second: float32 [768, 768], P('mp', 'dp'), may hold values from 6.958547e-13 to 1.1133676e-11
- expand_proj: float32 [768, 3072], P('dp', 'mp'), may hold values from -0.3247595 to 0.3247595
- expand_first: float32 [768, 3072], P('dp', 'mp'), may hold values from -2.670288e-05 to 2.670288e-05
- expand_second: float32 [768, 3072], P('dp', 'mp'), may hold values from 6.958547e-13 to 1.1133676e-11
- shrink_proj: float32 [3072, 768], P('mp', 'dp'), may hold values from -0.109375 to 0.109375
- shrink_first: float32 [3072, 768], P('mp', 'dp'), may hold values from -2.670288e-05 to 2.670288e-05
- shrink_second: float32 [3072, 768], P('mp', 'dp'), may hold values from 6.958547e-13 to 1.1133676e-11
- vectors: float32 [12, 768], P(None, ('dp', 'mp')), may hold values from -0.9 to 2.7, as said below
- vector_first: float32 [12, 768], P(None, ('dp', 'mp')), may hold values from -5.340576e-05 to 5.340576e-05
- vector_second: float32 [12, 768], P(None, ('dp', 'mp')), may hold values from 2.783419e-12 to 4.4534702e-11
Outputs:
- layer_output: bfloat16 [24576, 768], P('dp')
- input_grad: bfloat16 [24576, 768], P('dp')
- grad_norm: float32 [], replicated
- attn_mean: float32 [3, 768, 768], P(None, 'dp', 'mp')
- attn_square: float32 [3, 768, 768], P(None, 'dp', 'mp')
- attn_master: float32 [3, 768, 768], P(None, 'dp', 'mp')
- attn_copy: bfloat16 [3, 768, 768], P(None, 'dp', 'mp')
- box_mean: float32 [128, 768], P('dp', 'mp')
- box_square: float32 [128, 768], P('dp', 'mp')
- box_master: float32 [128, 768], P('dp', 'mp')
- box_copy: bfloat16 [128, 768], P('dp', 'mp')
- merge_mean: float32 [768, 768], P('mp', 'dp')
- merge_square: float32 [768, 768], P('mp', 'dp')
- merge_master: float32 [768, 768], P('mp', 'dp')
- merge_copy: bfloat16 [768, 768], P('mp', 'dp')
- expand_mean: float32 [768, 3072], P('dp', 'mp')
- expand_square: float32 [768, 3072], P('dp', 'mp')
- expand_master: float32 [768, 3072], P('dp', 'mp')
- expand_copy: bfloat16 [768, 3072], P('dp', 'mp')
- shrink_mean: float32 [3072, 768], P('mp', 'dp')
- shrink_square: float32 [3072, 768], P('mp', 'dp')
- shrink_master: float32 [3072, 768], P('mp', 'dp')
- shrink_copy: bfloat16 [3072, 768], P('mp', 'dp')
- vector_mean: float32 [12, 768], P(None, ('dp', 'mp'))
- vector_square: float32 [12, 768], P(None, ('dp', 'mp'))
- vector_master: float32 [12, 768], P(None, ('dp', 'mp'))
Inputs may be any that keep to these rules, and one draw needn't show every extreme that they name: `vectors`: norm gains are positive.
All inputs are finite; a program needn't handle non-finite values.
Results may differ from a plain program's by a relative error of at most 0.019.
Values may be sent and summed in bfloat16 or wider, within the bound.
A program may use at most 192 MiB of HBM per device.

v0:
```python
import functools
import types

import jax
import jax.numpy as jnp
import numpy as np
from jax import lax
from jax.experimental import pallas as pl
from jax.experimental.pallas import tpu as pltpu
from jax.sharding import PartitionSpec as P

HD = 64
FREQS = 32
PE = 128
PAGE = 512
STEP = 10

NORM_EPS = 1e-12
CLIP_LIMIT = 0.1
BETA_ONE = 0.9
BETA_TWO = 0.999
ADAM_EPS = 1e-08
RATE_MATRIX = 0.05
RATE_VECTOR = 0.5
WEIGHT_DECAY = 0.01

F32 = jnp.float32
BF16 = jnp.bfloat16
VMEM_LIMIT = 60 * 1024 * 1024

NN = (((1,), (0,)), ((), ()))
NT = (((1,), (1,)), ((), ()))
TN = (((0,), (0,)), ((), ()))


def dot(lhs, rhs, dims=NN):
    return lax.dot_general(lhs, rhs, dims, preferred_element_type=F32)


def aligned(index, size):
    return pl.ds(pl.multiple_of(index * size, size), size)


def swap_blocks(feat):
    return jnp.concatenate(
        [
            feat[FREQS : 2 * FREQS],
            feat[0:FREQS],
            feat[3 * FREQS :],
            feat[2 * FREQS : 3 * FREQS],
        ],
        axis=0,
    )


def turn_factors(trig):
    cos_x, sin_x = trig[0:FREQS], trig[FREQS : 2 * FREQS]
    cos_y, sin_y = trig[2 * FREQS : 3 * FREQS], trig[3 * FREQS :]
    return (
        jnp.concatenate([sin_x, sin_x, sin_y, sin_y], axis=0),
        jnp.concatenate([cos_x, -cos_x, cos_y, -cos_y], axis=0),
    )


MESH = pl.DeviceIdType.MESH
ALL = slice(None)
UNIT = 384


class Place:
    def __init__(self):
        rank = lax.axis_index("dp")
        self.m = lax.axis_index("mp")
        self.z = rank // 4
        self.y = (rank // 2) % 2
        self.c = rank % 2
        self.peer = {
            "x": (rank, 1 - self.m),
            "y": (rank + 2 - 4 * self.y, self.m),
            "c": (rank + 1 - 2 * self.c, self.m),
        }
        self.far = [((rank + 4 * step) % 16, self.m) for step in (1, 2, 3)]

    def signal(self):
        barrier = pltpu.get_barrier_semaphore()
        for device in list(self.peer.values()) + self.far:
            pl.semaphore_signal(barrier, inc=1, device_id=device, device_id_type=MESH)

    def wait(self):
        pl.semaphore_wait(pltpu.get_barrier_semaphore(), 6)

    def signal_all(self):
        barrier = pltpu.get_barrier_semaphore()
        rank = self.m * 16 + lax.axis_index("dp")

        def one(step, carry):
            to = (rank + step) % 32
            pl.semaphore_signal(barrier, inc=1, device_id=(to % 16, to // 16), device_id_type=MESH)
            return carry

        lax.fori_loop(1, 32, one, 0)

    def wait_all(self):
        pl.semaphore_wait(pltpu.get_barrier_semaphore(), 31)


PART = 256


def start_rows(src, dst, rows, send_sem, recv_sem, device):
    for first in range(0, rows, PART):
        part = pl.ds(first, PART)
        remote(src.at[part, :], dst.at[part, :], send_sem, recv_sem, device).start()


def remote(src, dst, send_sem, recv_sem, device):
    return pltpu.make_async_remote_copy(
        src_ref=src,
        dst_ref=dst,
        send_sem=send_sem,
        recv_sem=recv_sem,
        device_id=device,
        device_id_type=MESH,
    )


SLOT = {"c": 0, "z": 1, "y": 4, "x": 5}
SLOTS = 6
SENT = (0, 1, 1, 1, 4, 5)


class Tree:
    lag = 1
    held_back = 0
    together = False

    def stage(self, index, chunk):
        raise NotImplementedError

    def event(self, number):
        for index in range(self.count - 1 - self.held_back, -1, -1):
            chunk = number - index * self.lag
            if self.together:

                @pl.when(chunk == 0)
                def _(index=index):
                    for each in range(self.chunks):
                        self.stage(index, each)

            elif self.chunks == 1:
                pl.when(chunk == 0)(lambda index=index: self.stage(index, 0))
            else:
                pl.when((chunk >= 0) & (chunk < self.chunks))(
                    lambda index=index, chunk=chunk: self.stage(index, chunk)
                )

    @property
    def events(self):
        return self.chunks + (self.count - 1 - self.held_back) * self.lag

    def rest(self):
        def one(chunk, carry):
            self.stage(self.count - 1, chunk)
            return carry

        lax.fori_loop(0, self.chunks, one, 0)


class Spread(Tree):
    def __init__(self, place, ref, chunks, order, sems):
        self.chunks, self.ref, self.sems, self.place = chunks, ref, sems, place
        have = {"x": place.m if "x" in order else 0, "z": place.z, "y": place.y}
        mine = {"x": place.m, "y": place.y}
        self.own = have
        self.steps, self.axes = [], order
        for axis in order:
            if axis == "z":
                sends = [(have, place.far[step - 1], step) for step in (1, 2, 3)]
                waits = [(dict(have, z=(place.z + 4 - step) % 4), step) for step in (1, 2, 3)]
            else:
                sends = [(have, place.peer[axis], SLOT[axis])]
                waits = [(dict(have, **{axis: 1 - mine[axis]}), SLOT[axis])]
            self.steps.append((sends, waits))
            have = dict(have, **{axis: ALL})
        self.other = place.peer["c"]
        self.count = len(self.steps) + 2

    def _copy(self, chunk, have, device, slot):
        came = 0 if chunk == ALL else chunk
        block = self.ref.at[chunk, self.place.c, have["x"], have["z"], have["y"]]
        sent = self.sems.at[0, 0, SENT[slot]]
        return remote(block, block, sent, self.sems.at[1, came, slot], device)

    def _plane(self, chunk, core):
        plane = self.ref.at[chunk, core]
        came = 0 if chunk == ALL else chunk
        return remote(plane, plane, self.sems.at[0, 0, 0], self.sems.at[1, came, 0], self.other)

    def stage(self, index, chunk):
        if index == self.count - 1:
            self._plane(chunk, 1 - self.place.c).wait_recv()
            return
        came = [self.own]
        if index > 0:
            came = []
            for have, slot in self.steps[index - 1][1]:
                self._copy(chunk, have, self.other, slot).wait_recv()
                came.append(have)
        if index < len(self.steps):
            for have, device, slot in self.steps[index][0]:
                self._copy(chunk, have, device, slot).start()
        for have in came:
            self._copy(chunk, have, self.other, 0).start()

    def drain(self):
        for axis, (sends, _) in zip(self.axes, self.steps):
            have, _, slot = sends[0]
            if axis == "z":
                have = dict(have, z=slice(0, 3))
            self._copy(ALL, have, self.other, slot).wait_send()
        self._plane(ALL, self.place.c).wait_send()


RANKS = [(c, z, y) for z in range(4) for y in range(2) for c in range(2)]


def natural(ref, chunk, side):
    return jnp.concatenate([ref[chunk, c, side, z, y] for c, z, y in RANKS], axis=0)


def put_natural(ref, chunk, side, value):
    rows = value.shape[0] // len(RANKS)
    for spot, (c, z, y) in enumerate(RANKS):
        ref[chunk, c, side, z, y] = value[spot * rows : (spot + 1) * rows]


class Reduce(Tree):
    def __init__(self, place, full, total, lands, chunks, order, sems, finish):
        self.place, self.full, self.total, self.lands = place, full, total, lands
        self.chunks, self.sems, self.finish = chunks, sems, finish
        mine = {"x": place.m, "y": place.y}
        self.across = ALL if "x" in order else 0
        have = {"x": self.across, "z": ALL, "y": ALL}
        self.order, self.haves = order, []
        for axis in order:
            before = have
            if axis != "c":
                have = dict(have, **{axis: place.z if axis == "z" else mine[axis]})
            self.haves.append((before, have))
        self.count = len(order) + 1

    def _at(self, chunk, have):
        if self.total is None:
            return self.full.at[chunk, self.place.c, have["x"], have["z"], have["y"]]
        return self.total.at[chunk, have["x"], have["z"], have["y"]]

    def _copies(self, index, chunk):
        axis, (before, _) = self.order[index], self.haves[index]
        place, land = self.place, self.lands[axis]

        def copy(src, dst, slot, device):
            return remote(src, dst, self.sems.at[0, 0, SENT[slot]], self.sems.at[1, chunk, slot], device)

        if axis == "c":
            source = self.full.at[chunk, 1 - place.c, self.across]
            return [copy(source, land.at[chunk], SLOT[axis], place.peer[axis])]
        if axis == "z":
            return [
                copy(
                    self._at(chunk, dict(before, z=(place.z + step) % 4)),
                    land.at[chunk, step - 1],
                    step,
                    place.far[step - 1],
                )
                for step in (1, 2, 3)
            ]
        other = 1 - (place.m if axis == "x" else place.y)
        source = self._at(chunk, dict(before, **{axis: other}))
        return [copy(source, land.at[chunk], SLOT[axis], place.peer[axis])]

    def stage(self, index, chunk):
        if index > 0:
            axis, (_, have) = self.order[index - 1], self.haves[index - 1]
            land = self.lands[axis]
            for copy in self._copies(index - 1, chunk):
                copy.wait_recv()
            mine = self._at(chunk, have)
            last = index == self.count - 1
            if axis == "z":
                value = mine[...].astype(F32)
                for step in range(3):
                    value += land[chunk, step].astype(F32)
            elif last:
                value = mine[...].astype(F32) + land[chunk].astype(F32)
            else:
                value = mine[...] + land[chunk]
            if last:
                self.finish(chunk, value)
            else:
                mine[...] = value.astype(mine.dtype)
        if index < self.count - 1:
            for copy in self._copies(index, chunk):
                copy.start()

    def drain(self):
        for axis in self.order:
            land = self.lands[axis]
            slot = SLOT[axis]
            sent = self.sems.at[0, 0, SENT[slot]]
            remote(land, land, sent, self.sems.at[1, 0, slot], self.place.peer["c"]).wait_send()


class Everyone:
    def __init__(self, place, send_block, land_block, sems):
        self.rank = place.m * 16 + lax.axis_index("dp")
        self.send_block, self.land_block, self.sems = send_block, land_block, sems

    def _copy(self, step):
        to = (self.rank + step) % 32
        return remote(
            self.send_block(to),
            self.land_block(step),
            self.sems.at[0, step - 1],
            self.sems.at[1, step - 1],
            (to % 16, to // 16),
        )

    def _each(self, act):
        def one(step, carry):
            act(self._copy(step))
            return carry

        lax.fori_loop(1, 32, one, 0)

    def start(self):
        self._each(lambda copy: copy.start())

    def wait(self):
        self._each(lambda copy: copy.wait())


VROWS = 16


def rows_from_blocks(blocks, pick, counts):
    mp_count, dp_count = counts
    width = pick.shape[1]
    each = width // (mp_count * dp_count)
    wide = lax.dot_general(
        blocks, pick, NN, precision=lax.Precision.HIGHEST, preferred_element_type=F32
    )
    lane = lax.broadcasted_iota(jnp.int32, (VROWS, width), 1)
    table = jnp.zeros((VROWS, width), F32)
    for m in range(mp_count):
        for r, (c, z, y) in enumerate(RANKS):
            first = (r * mp_count + m) * each
            row = (((c * mp_count + m) * 4 + z) * 2 + y) * VROWS
            table += jnp.where((lane >= first) & (lane < first + each), wide[row : row + VROWS], 0.0)
    return table


def attend_setup(heads, m, box_full, vec_ref, box_heads, bias):
    cols = heads * HD
    for head in range(heads):
        box_heads[head] = box_full[:, head * HD : (head + 1) * HD]
    width = vec_ref.shape[1]
    own = jnp.where(m == 0, vec_ref[6:8, 0:cols], vec_ref[6:8, width - cols :])
    spread = exact_dot(jnp.broadcast_to(own[1:2], (8, cols)), pair_place(cols))
    bias[0:1, 0:cols] = own[0:1]
    bias[0:1, cols:] = spread[0:1]


def attend_trig(omega_ref, corner_ref, trig_ref):
    corner = corner_ref[...].astype(F32)
    angle_x = omega_ref[...] * ((corner[0:1] + corner[2:3]) * 0.5)
    angle_y = omega_ref[...] * ((corner[1:2] + corner[3:4]) * 0.5)
    trig_ref[0:FREQS, :] = jnp.cos(angle_x)
    trig_ref[FREQS : 2 * FREQS, :] = jnp.sin(angle_x)
    trig_ref[2 * FREQS : 3 * FREQS, :] = jnp.cos(angle_y)
    trig_ref[3 * FREQS :, :] = jnp.sin(angle_y)


def quiet(*args):
    return None


def attend_math(heads, r, weights, page_of, projected, attended):
    cols = heads * HD
    pages = r.x.shape[0] // PAGE

    def project(page, carry):
        rows = aligned(page, PAGE)
        tokens = r.x[rows, :]
        query = dot(tokens, weights(0)) + r.bias[0:1, 0:cols]
        query = query.astype(BF16) * HD ** (-0.5)
        r.qtok[rows, :] = query
        qa_rows = query.T
        for half in range(2):
            lanes = slice(half * cols, (half + 1) * cols)
            pair = dot(tokens, weights(1 + half)) + r.bias[0:1, cols + half * cols : 2 * cols + half * cols]
            pair = pair.astype(BF16)
            r.kvtok[rows, lanes] = pair
            turned = pair.T
            for spot in range(heads // 2):
                head_rows = slice((half * heads // 2 + spot) * HD, (half * heads // 2 + spot + 1) * HD)
                r.kt[head_rows, rows] = turned[2 * spot * HD : (2 * spot + 1) * HD]
                r.vt[head_rows, rows] = turned[(2 * spot + 1) * HD : (2 * spot + 2) * HD]
        trig = r.trig[:, rows]
        kft = trig.astype(BF16)
        r.kft[:, rows] = kft
        r.kftok[rows, :] = kft.T
        own, partner = turn_factors(trig)
        for head in range(heads):
            query_head = qa_rows[head * HD : (head + 1) * HD]
            proj = dot(r.box_heads[head], query_head)
            feat = proj * own + swap_blocks(proj) * partner
            r.qa[head, 0:PE, rows] = feat.astype(BF16)
            r.qa[head, PE : PE + HD, rows] = query_head
        projected(page)
        return carry

    lax.fori_loop(0, pages, project, 0)

    def attend(step, carry):
        turn, pair = step // (heads // 2), step % (heads // 2)
        rows = aligned(page_of(turn), PAGE)
        halves = []
        blank = jnp.zeros((HD, PAGE), BF16)
        for side in range(2):
            head = pair * 2 + side
            lanes = aligned(head, 2 * HD)
            left = jnp.concatenate([r.kftok[rows, :], r.kvtok[rows, lanes]], axis=1)
            score = dot(left, jnp.concatenate([r.qa[head, :, rows], blank], axis=0))
            top = jnp.max(score, axis=0, keepdims=True)
            weight = jnp.exp(score - top)
            total = jnp.sum(weight, axis=0, keepdims=True)
            value = r.vt[aligned(head, HD), rows]
            halves.append(dot(value, weight.astype(BF16)) * (1.0 / total))
            r.log[head, :, rows] = top + jnp.log(total)
        both = jnp.concatenate(halves, axis=0).astype(BF16)
        lanes = aligned(pair, 2 * HD)
        r.ctxt[lanes, rows] = both
        r.ctx[rows, lanes] = both.T
        attended(step, turn, pair)
        return carry

    lax.fori_loop(0, pages * (heads // 2), attend, 0)


def attend_buffers(heads, tokens):
    cols = heads * HD
    kept = [
        ("qa", (heads, PE + HD, tokens), BF16),
        ("qtok", (tokens, cols), BF16),
        ("kvtok", (tokens, 2 * cols), BF16),
        ("kt", (cols, tokens), BF16),
        ("kft", (PE, tokens), BF16),
        ("trig", (PE, tokens), F32),
        ("ctxt", (cols, tokens), BF16),
        ("log", (heads, 1, tokens), F32),
    ]
    used = [
        ("kftok", (tokens, PE), BF16),
        ("box_heads", (heads, PE, HD), BF16),
        ("bias", (8, 3 * cols), F32),
        ("ctx", (tokens, cols), BF16),
        ("vt", (cols, tokens), BF16),
    ]
    return kept, used


def attend_kernel(heads, names, *refs):
    r = types.SimpleNamespace(**dict(zip(names, refs)))
    attend_setup(heads, lax.axis_index("mp"), r.box, r.vec, r.box_heads, r.bias)
    attend_trig(r.omega, r.corner, r.trig)
    attend_math(heads, r, lambda chunk: r.w[chunk], lambda turn: turn, quiet, quiet)


def attend_forward(x, corners, omega, w_qkv, w_box, vecs):
    tokens = x.shape[0]
    heads = w_box.shape[1] // HD
    kept, used = attend_buffers(heads, tokens)
    outs = kept + [used[3]]
    scratch = used[:3] + used[4:]
    names = ["x", "corner", "omega", "w", "box", "vec"] + [item[0] for item in outs + scratch]
    vmem = pl.BlockSpec(memory_space=pltpu.VMEM)
    return pl.pallas_call(
        functools.partial(attend_kernel, heads, names),
        out_shape=[jax.ShapeDtypeStruct(shape, kind) for _, shape, kind in outs],
        in_specs=[vmem] * 6,
        out_specs=[vmem] * len(outs),
        scratch_shapes=[pltpu.VMEM(shape, kind) for _, shape, kind in scratch],
        compiler_params=pltpu.CompilerParams(vmem_limit_bytes=VMEM_LIMIT),
        name="attend_forward",
    )(x, corners, omega, w_qkv, w_box, vecs)


TILE = 256


def normal_parts(value):
    phi = 0.5 + 0.5 * lax.erf(value * 2.0 ** (-0.5))
    return phi, phi + value * (jnp.exp(value * value * -0.5) * (0.5 / np.pi) ** 0.5)


def norm_stats(value):
    mean = jnp.mean(value, axis=-1, keepdims=True)
    centred = value - mean
    var = jnp.mean(centred * centred, axis=-1, keepdims=True)
    return centred, lax.rsqrt(var + NORM_EPS)


def norm_back(grad_normed, normed, scale):
    first = jnp.mean(grad_normed, axis=-1, keepdims=True)
    second = jnp.mean(grad_normed * normed, axis=-1, keepdims=True)
    return scale * (grad_normed - first - normed * second)


def col_sum(value):
    return jnp.sum(value, axis=0, keepdims=True)


def feed_math(r, hooks):
    hook = {name: quiet for name in ("entered", "grew", "turned", "shrinks", "shrank", "left", "expands")}
    hook.update(hooks)
    tokens = r.x.shape[0]
    sides = r.ctxx.shape[0]
    steps = r.ws.shape[0]
    tiles = tokens // TILE
    wide = sides * UNIT
    sum2 = dnorm = r.sum2

    def flat(ref, chunk, side):
        return ref[chunk, side] if len(ref.shape) == 4 else natural(ref, chunk, side)

    def put(ref, chunk, side, value):
        if len(ref.shape) == 4:
            ref[chunk, side] = value
        else:
            put_natural(ref, chunk, side, value)

    def lay_out(step):
        for plain, ref, chunk in ((r.plain_e, r.we, 1 + step), (r.plain_s, r.ws, step)):
            for side in range(sides):
                lanes = slice(side * UNIT, (side + 1) * UNIT)
                if len(ref.shape) == 4:
                    plain[:, lanes] = ref[chunk, side]
                else:
                    rows = plain.shape[0] // len(RANKS)
                    for spot, (c, z, y) in enumerate(RANKS):
                        plain[spot * rows : (spot + 1) * rows, lanes] = ref[chunk, c, side, z, y]

    def put_both(ref, chunk, value):
        for side in range(sides):
            put(ref, chunk, side, value[:, side * UNIT : (side + 1) * UNIT])

    def bias_at(step, side):
        first = side * steps + step
        return (pl.ds(8 + first // 2, 1), aligned(first % 2, UNIT))

    def enter(tile, carry):
        rows = aligned(tile, TILE)
        total = r.x[rows, :].astype(F32) + r.vec[4:5, :]
        for side in range(sides):
            total += dot(r.ctxx[side, rows, :], flat(r.we, 0, side), NT)
        centred, scale = norm_stats(total)
        normed = centred * scale
        r.norm1[rows, :] = normed
        r.scale1[rows, :] = scale
        shifted = normed * r.vec[0:1, :] + r.vec[1:2, :]
        r.al[rows, :] = shifted.astype(BF16)
        sum2[rows, :] = shifted + r.vec[5:6, :]
        return carry

    lax.fori_loop(0, tiles, enter, 0)
    hook["entered"]()

    def grow(step, carry):
        whole = aligned(step, wide)
        bias = jnp.concatenate([r.vec[bias_at(step, side)] for side in range(sides)], axis=1)
        lay_out(step)

        def one(tile, inner):
            rows = aligned(tile, TILE)
            pre = dot(r.al[rows, :], r.plain_e[...]) + bias
            phi, slope = normal_parts(pre)
            low = (pre * phi).astype(BF16)
            r.act[rows, whole] = low
            r.slope[rows, whole] = slope.astype(BF16)
            sum2[rows, :] += dot(low, r.plain_s[...], NT)
            hook["grew"](step * tiles + tile)
            return inner

        lax.fori_loop(0, tiles, one, 0)
        return carry

    lax.fori_loop(0, steps, grow, 0)
    r.vsum[...] = jnp.zeros_like(r.vsum)

    def turn(tile, carry):
        rows = aligned(tile, TILE)
        centred, scale = norm_stats(sum2[rows, :])
        normed = centred * scale
        r.out[rows, :] = (normed * r.vec[2:3, :] + r.vec[3:4, :]).astype(BF16)
        grad = r.og[rows, :].astype(F32)
        r.vsum[2:3, :] += col_sum(grad * normed)
        r.vsum[3:4, :] += col_sum(grad)
        back = norm_back(grad * r.vec[2:3, :], normed, scale)
        r.vsum[5:6, :] += col_sum(back)
        r.dh2l[rows, :] = back.astype(BF16)
        dnorm[rows, :] = back
        hook["turned"](tile)
        return carry

    lax.fori_loop(0, tiles, turn, 0)
    r.flip[...] = r.dh2l[...].T

    def grad_shrink(step, carry):
        grad = dot(r.flip[...], r.act[:, aligned(step, wide)]).astype(BF16)
        put_both(r.gs, step, grad)
        hook["shrinks"](step)
        return carry

    lax.fori_loop(0, steps, grad_shrink, 0)

    def shrink(step, carry):
        whole = aligned(step, wide)
        lay_out(step)

        def one(tile, inner):
            rows = aligned(tile, TILE)
            grad = dot(r.dh2l[rows, :], r.plain_s[...])
            low = (grad * r.slope[rows, whole].astype(F32)).astype(BF16)
            r.slope[rows, whole] = low
            sums = col_sum(low.astype(F32))
            for side in range(sides):
                r.vsum[bias_at(step, side)] += sums[:, side * UNIT : (side + 1) * UNIT]
            dnorm[rows, :] += dot(low, r.plain_e[...], NT)
            hook["shrank"](step * tiles + tile)
            return inner

        lax.fori_loop(0, tiles, one, 0)
        return carry

    lax.fori_loop(0, steps, shrink, 0)

    def leave(tile, carry):
        rows = aligned(tile, TILE)
        grad = dnorm[rows, :]
        normed = r.norm1[rows, :]
        r.vsum[0:1, :] += col_sum(grad * normed)
        r.vsum[1:2, :] += col_sum(grad)
        back = norm_back(grad * r.vec[0:1, :], normed, r.scale1[rows, :])
        r.vsum[4:5, :] += col_sum(back)
        low = back.astype(BF16)
        r.dh1l[rows, :] = low
        for side in range(sides):
            r.dctx[side, rows, :] = dot(low, flat(r.we, 0, side)).astype(BF16)
        hook["left"](tile)
        return carry

    lax.fori_loop(0, tiles, leave, 0)
    r.flip[...] = r.al[...].T

    def grad_expand(step, carry):
        grad = dot(r.flip[...], r.slope[:, aligned(step, wide)]).astype(BF16)
        put_both(r.ge, 1 + step, grad)
        hook["expands"](step)
        return carry

    lax.fori_loop(0, steps, grad_expand, 0)
    r.flip[...] = r.dh1l[...].T
    for side in range(sides):
        put(r.ge, 0, side, dot(r.flip[...], r.ctxx[side]).astype(BF16))


def feed_buffers(tokens, width, hidden):
    return [
        ("norm1", (tokens, width), F32),
        ("scale1", (tokens, 1), F32),
        ("sum2", (tokens, width), F32),
        ("al", (tokens, width), BF16),
        ("act", (tokens, hidden), BF16),
        ("slope", (tokens, hidden), BF16),
        ("dh2l", (tokens, width), BF16),
        ("flip", (width, tokens), BF16),
        ("plain_e", (width, 2 * UNIT), BF16),
        ("plain_s", (width, 2 * UNIT), BF16),
    ]


def feed_kernel(names, *refs):
    feed_math(types.SimpleNamespace(**dict(zip(names, refs))), {})


def feed_both(x, og, ctx, w_expand, w_shrink, vecs):
    tokens, width = x.shape
    chunks, sides = w_shrink.shape[0:2]
    outs = [
        ("out", (tokens, width), BF16),
        ("dctx", (sides, tokens, UNIT), BF16),
        ("dh1l", (tokens, width), BF16),
        ("ge", (chunks + 1, sides, width, UNIT), BF16),
        ("gs", (chunks, sides, width, UNIT), BF16),
        ("vsum", (VROWS, width), F32),
    ]
    scratch = feed_buffers(tokens, width, sides * chunks * UNIT)
    names = ["x", "og", "ctxx", "we", "ws", "vec"] + [item[0] for item in outs + scratch]
    vmem = pl.BlockSpec(memory_space=pltpu.VMEM)
    return pl.pallas_call(
        functools.partial(feed_kernel, names),
        out_shape=[jax.ShapeDtypeStruct(shape, kind) for _, shape, kind in outs],
        in_specs=[vmem] * 6,
        out_specs=[vmem] * len(outs),
        scratch_shapes=[pltpu.VMEM(shape, kind) for _, shape, kind in scratch],
        compiler_params=pltpu.CompilerParams(vmem_limit_bytes=VMEM_LIMIT),
        name="feed_both",
    )(x, og, ctx, w_expand, w_shrink, vecs)


def layer_kernel(heads, plan, inv_tokens, names, kept, used, feeds, *refs):
    r = types.SimpleNamespace(**dict(zip(names, refs)))
    cols = heads * HD
    tokens = r.x_all.shape[0]
    pages = tokens // PAGE
    own_tokens = tokens // 2
    tiles = own_tokens // TILE
    place = Place()
    place.signal()
    m, peer = place.m, place.peer["x"]
    at = (place.z, place.y)
    own = aligned(m, own_tokens)
    load_x = pltpu.make_async_copy(r.x_all.at[own, :], r.x, r.load_sem.at[0])
    load_og = pltpu.make_async_copy(r.og_all.at[own, :], r.og, r.load_sem.at[1])
    load_x.start()
    load_og.start()
    r.w[(0, place.c, 0, *at)] = r.attn[0].astype(BF16)
    for half in range(2):
        r.w[(1 + half, place.c, 0, *at)] = jnp.concatenate(
            [
                r.attn[1 + kind, :, head * HD : (head + 1) * HD].astype(BF16)
                for head in range(half * heads // 2, (half + 1) * heads // 2)
                for kind in range(2)
            ],
            axis=1,
        )
    r.box_gather[(0, place.c, 0, *at)] = r.shard_box[...]
    r.vec_gather[(0, place.c, m, *at)] = jnp.zeros((VROWS, 128), F32)
    table_at = (slice(0, r.vectors.shape[0]), slice(0, r.vectors.shape[1]))
    r.vec_gather[(0, place.c, m, *at, *table_at)] = r.vectors[...]
    r.we[(0, place.c, m, *at)] = r.merge[...].astype(BF16)
    for chunk in range(4):
        lanes = slice(chunk * UNIT, (chunk + 1) * UNIT)
        r.we[(1 + chunk, place.c, m, *at)] = r.expand[:, lanes].astype(BF16)
        r.ws[(chunk, place.c, m, *at)] = r.shrink[:, lanes].astype(BF16)
    place.wait()
    tree_v = Spread(place, r.vec_gather, 1, "xzy", r.v_sem)
    tree_b = Spread(place, r.box_gather, 1, "zy", r.b_sem)
    tree_a = Spread(place, r.w, 3, "zy", r.a_sem)
    tree_e = Spread(place, r.we, 5, "zyx", r.e_sem)
    tree_f = Spread(place, r.ws, 4, "xzy", r.f_sem)
    tree_e.lag = tree_f.lag = 2
    first, late = tree_a.events, 3
    begun = first - late

    def weights_event(number):
        tree_e.event(number)
        tree_f.event(number)

    def finish(chunk, value):
        r.sum_f[chunk] = value * inv_tokens

    back_f = Reduce(
        place, r.gs, None, dict(c=r.fc, y=r.fy, z=r.fz, x=r.fx), 4, "cyzx", r.back_sem, finish
    )
    back_f.lag, back_f.held_back = 2, 1

    def attention(*scoped):
        q = types.SimpleNamespace(**dict(zip([item[0] for item in kept + used] + ["x", "plain_w"], scoped)))
        load_all = pltpu.make_async_copy(r.x_all, q.x, r.load_sem.at[2])
        load_all.start()

        tree_v.stage(0, 0)

        def begin(number, carry):
            tree_v.event(number + 1)
            tree_b.event(number)

            @pl.when(number == 4)
            def _():
                r.vec[...] = rows_from_blocks(
                    r.vec_gather[...].reshape(-1, 128), r.pick[...], plan
                )
                r.box_out[...] = natural(r.box_gather, 0, 0).astype(BF16)
                attend_setup(heads, m, r.box_out, r.vec, q.box_heads, q.bias)

            tree_a.event(number)
            weights_event(number - late)
            pl.when(number == 0)(lambda: attend_trig(r.omega, r.corner, q.trig))
            return carry

        lax.fori_loop(0, first, begin, 0)
        for chunk in range(3):
            q.plain_w[chunk] = natural(r.w, chunk, 0)
        keep_w = pltpu.make_async_copy(q.plain_w, r.w_out, r.load_sem.at[3])
        keep_w.start()
        load_all.wait()

        def projected(page):
            pl.when(page < 2)(lambda: weights_event(begun + page))

        piece = PAGE // 2

        def swap_copy(index):
            theirs = pages * (1 - m) + index
            start_rows(
                q.ctx.at[aligned(theirs, piece), :],
                r.ctxx.at[m, aligned(index, piece), :],
                piece,
                r.ctx_sem.at[0, index],
                r.ctx_sem.at[1, index],
                peer,
            )

        def attended(step, turn, pair):
            pl.when(step % 3 == 1)(lambda: weights_event(begun + 2 + step // 3))
            pl.when(step == 8)(lambda: weights_event(begun + 5))

            @pl.when(step == heads // 2 - 1)
            def _():
                swap_copy(2 - 2 * m)
                swap_copy(1)

            @pl.when(step == heads - 1)
            def _():
                swap_copy(2 * m)

        attend_math(
            heads,
            q,
            lambda chunk: q.plain_w[chunk],
            lambda turn: turn * m + (pages - 1 - turn) * (1 - m),
            projected,
            attended,
        )
        stores = [
            pltpu.make_async_copy(getattr(q, name), getattr(r, name + "_out"), r.store_sem.at[k])
            for k, (name, _, _) in enumerate(kept)
        ]
        for copy in stores:
            copy.start()
        r.ctxx[m] = q.ctx[own, :]
        for index in range(pages):
            copy = remote(
                q.ctx.at[aligned(index, piece), :],
                r.ctxx.at[1 - m, aligned(index, piece), :],
                r.ctx_sem.at[0, index],
                r.ctx_sem.at[1, index],
                peer,
            )
            copy.wait_recv()
            copy.wait_send()
        for copy in stores:
            copy.wait()
        keep_w.wait()

    pl.run_scoped(
        attention,
        *[pltpu.VMEM(shape, kind) for _, shape, kind in kept + used],
        pltpu.VMEM(r.x_all.shape, BF16),
        pltpu.VMEM(r.w_out.shape, BF16),
    )

    def feed(*scoped):
        q = types.SimpleNamespace(**dict(zip([item[0] for item in feeds], scoped)))
        for name in ("x", "og", "we", "ws", "vec", "ctxx", "dh1l", "ge", "gs", "vsum"):
            setattr(q, name, getattr(r, name))

        def out_copies(tile):
            rows = aligned(tile, TILE)
            there = r.out_full.at[pl.ds(pl.multiple_of(m * own_tokens + tile * TILE, TILE), TILE), :]
            return (
                pltpu.make_async_copy(q.out.at[rows, :], there, r.swap_sem.at[0, tile]),
                remote(q.out.at[rows, :], there, r.swap_sem.at[1, tile], r.swap_sem.at[2, tile], peer),
            )

        def dctx_copies(tile):
            rows = aligned(tile, TILE)
            there = r.dctx_full.at[pl.ds(pl.multiple_of(m * own_tokens + tile * TILE, TILE), TILE), :]
            return (
                pltpu.make_async_copy(q.dctx.at[m, rows, :], there, r.swap_sem.at[3, tile]),
                remote(
                    q.dctx.at[1 - m, rows, :], there, r.swap_sem.at[4, tile], r.swap_sem.at[5, tile], peer
                ),
            )

        def start_out(tile):
            rows = aligned(tile, TILE)
            there = r.out_full.at[pl.ds(pl.multiple_of(m * own_tokens + tile * TILE, TILE), TILE), :]
            out_copies(tile)[0].start()
            sems = r.swap_sem.at[1, tile], r.swap_sem.at[2, tile]
            start_rows(q.out.at[rows, :], there, TILE, *sems, peer)

        def start_dctx(tile):
            rows = aligned(tile, TILE)
            there = r.dctx_full.at[pl.ds(pl.multiple_of(m * own_tokens + tile * TILE, TILE), TILE), :]
            dctx_copies(tile)[0].start()
            sems = r.swap_sem.at[4, tile], r.swap_sem.at[5, tile]
            start_rows(q.dctx.at[1 - m, rows, :], there, TILE, *sems, peer)

        def grew(number):
            pl.when(number % 3 == 1)(lambda: weights_event(begun + 7 + number // 3))

        def shrinks(step):
            pl.when(step != 2)(lambda: back_f.event(step - step // 3))

        def shrank(number):
            for spot, event in ((1, 3), (4, 4), (8, 5), (11, 6)):
                pl.when(number == spot)(lambda event=event: back_f.event(event))

        def expands(step):
            pl.when(step != 1)(lambda: back_f.event(7 + (step + 1) // 2))

        load_x.wait()
        load_og.wait()
        feed_math(
            q,
            dict(
                entered=lambda: weights_event(begun + 6),
                grew=grew,
                expands=expands,
                turned=start_out,
                shrinks=shrinks,
                shrank=shrank,
                left=start_dctx,
            ),
        )
        back_f.rest()
        back_f.drain()
        for tile in range(tiles):
            for copy in out_copies(tile) + dctx_copies(tile):
                copy.wait()

    pl.run_scoped(feed, *[pltpu.VMEM(shape, kind) for _, shape, kind in feeds])
    for tree in (tree_v, tree_b, tree_a, tree_e, tree_f):
        tree.drain()


def layer_forward(x, og, corners, omega, pick, shards, plan, inv_tokens):
    tokens, width = x.shape
    cols = shards[1].shape[1]
    heads = cols // HD
    own = tokens // 2
    unit = (width // 16, UNIT)
    kept, used = attend_buffers(heads, tokens)
    feeds = feed_buffers(own, width, 8 * UNIT)
    feeds += [("out", (own, width), BF16), ("dctx", (2, own, UNIT), BF16)]
    free = pl.BlockSpec(memory_space=pl.ANY)
    vmem = pl.BlockSpec(memory_space=pltpu.VMEM)
    inputs = [("x_all", free), ("og_all", free), ("corner", vmem), ("omega", vmem), ("pick", vmem)]
    inputs += [(name, vmem) for name in ("attn", "shard_box", "vectors", "merge", "expand", "shrink")]
    outs = [(name + "_out", shape, kind, free) for name, shape, kind in kept]
    outs += [
        ("w_out", (3, width, cols), BF16, free),
        ("box_out", (PE, cols), BF16, vmem),
        ("out_full", (tokens, width), BF16, free),
        ("dctx_full", (tokens, cols), BF16, free),
        ("dh1l", (own, width), BF16, vmem),
        ("ge", (5, 2, 2, 4, 2, *unit), BF16, vmem),
        ("vsum", (VROWS, width), F32, vmem),
        ("sum_f", (4, *unit), F32, vmem),
    ]
    dma = pltpu.SemaphoreType.DMA
    scratch = [
        ("x", pltpu.VMEM((own, width), BF16)),
        ("og", pltpu.VMEM((own, width), BF16)),
        ("vec", pltpu.VMEM((VROWS, width), F32)),
        ("w", pltpu.VMEM((3, 2, 1, 4, 2, *unit), BF16)),
        ("box_gather", pltpu.VMEM((1, 2, 1, 4, 2, PE // 16, cols), F32)),
        ("vec_gather", pltpu.VMEM((1, 2, 2, 4, 2, VROWS, 128), F32)),
        ("we", pltpu.VMEM((5, 2, 2, 4, 2, *unit), BF16)),
        ("ws", pltpu.VMEM((4, 2, 2, 4, 2, *unit), BF16)),
        ("ctxx", pltpu.VMEM((2, own, cols), BF16)),
        ("gs", pltpu.VMEM((4, 2, 2, 4, 2, *unit), BF16)),
        ("fc", pltpu.VMEM((4, 2, 4, 2, *unit), BF16)),
        ("fy", pltpu.VMEM((4, 2, 4, *unit), BF16)),
        ("fz", pltpu.VMEM((4, 3, 2, *unit), BF16)),
        ("fx", pltpu.VMEM((4, *unit), BF16)),
        ("ctx_sem", dma((2, 3))),
        ("a_sem", dma((2, 3, SLOTS))),
        ("b_sem", dma((2, 1, SLOTS))),
        ("v_sem", dma((2, 1, SLOTS))),
        ("e_sem", dma((2, 5, SLOTS))),
        ("f_sem", dma((2, 4, SLOTS))),
        ("back_sem", dma((2, 4, SLOTS))),
        ("load_sem", dma((4,))),
        ("store_sem", dma((len(kept),))),
        ("swap_sem", dma((6, own // TILE))),
    ]
    names = [item[0] for item in inputs + outs + scratch]
    return pl.pallas_call(
        functools.partial(layer_kernel, heads, plan, inv_tokens, names, kept, used, feeds),
        out_shape=[jax.ShapeDtypeStruct(shape, kind) for _, shape, kind, _ in outs],
        in_specs=[item[1] for item in inputs],
        out_specs=[item[3] for item in outs],
        scratch_shapes=[item[1] for item in scratch],
        compiler_params=pltpu.CompilerParams(
            vmem_limit_bytes=VMEM_LIMIT, collective_id=0, has_side_effects=True
        ),
        name="layer_forward",
    )(x, og, corners, omega, pick, *shards)


def pair_place(cols):
    spot = lax.broadcasted_iota(jnp.int32, (cols, 2 * cols), 0)
    lane = lax.broadcasted_iota(jnp.int32, (cols, 2 * cols), 1)
    target = ((spot >> 6) << 7) + HD + (spot & (HD - 1))
    return jnp.where(lane == target, 1.0, 0.0)


def exact_dot(lhs, rhs, dims=NN):
    return lax.dot_general(
        lhs, rhs, dims, precision=lax.Precision.HIGHEST, preferred_element_type=F32
    )


def attend_back_kernel(heads, plan, inv_tokens, *refs):
    inputs, refs = refs[:12], refs[12:]
    if plan is not None:
        load_sem, held, refs = refs[-1], refs[-13:-1], refs[:-13]
        loads = [
            pltpu.make_async_copy(src, dst, load_sem.at[k]) for k, (src, dst) in enumerate(zip(inputs, held))
        ]
        early = (0, 2, 7, 11)
        for k in sorted(range(12), key=lambda k: k not in early):
            loads[k].start()
        inputs = held
    x_ref, w_ref, box_ref, *inputs = inputs
    qa_ref, qtok_ref, kvtok_ref, kt_ref, kft_ref, trig_ref, ctxt_ref, log_ref, dctx_ref = inputs
    cols = heads * HD
    tokens = x_ref.shape[0]
    pages = tokens // PAGE
    m = lax.axis_index("mp")
    piece = PAGE // 2
    pieces = 2 * pages
    lane = lax.broadcasted_iota(jnp.int32, (1, 2 * HD), 1)
    lower = lane < HD
    if plan is None:
        inp_ref, gw_ref, gbox_ref, qvsum_ref, *refs = refs
        kftok, dctxt, boxt, dtok, xt, gbox = refs
        before, after = 0, 0

        def background(number):
            pass
    else:
        dh1_ref, vsum_ref, sumf_ref, pick_ref, full_e, *refs = refs
        inp_ref, sum_e, sum_a, sum_b, sum_v, norm_ref, *refs = refs
        kftok, dctxt, boxt, dtok, xt, gbox, *refs = refs
        came, total_e, full_a, full_b, full_v, land_v, norms, *refs = refs
        ec, ey, ez, ex, ac, ay, az, bc, by, bz, *refs = refs
        e_sem, a_sem, b_sem, v_sem, n_sem, i_sem, loc_sem = refs
        place = Place()
        place.signal_all()
        fill = pltpu.make_async_copy(full_e.at[:, place.c], total_e, loc_sem.at[0])
        fill.start()
        place.wait_all()

        def finish(out):
            def put(chunk, value):
                out[chunk] = value * inv_tokens

            return put

        tree_e = Reduce(
            place, full_e, total_e, dict(c=ec, y=ey, z=ez, x=ex), 5, "cyzx", e_sem, finish(sum_e)
        )
        tree_e.lag, tree_e.held_back = 2, 1
        tree_a = Reduce(place, full_a, None, dict(c=ac, y=ay, z=az), 3, "cyz", a_sem, finish(sum_a))
        tree_b = Reduce(place, full_b, None, dict(c=bc, y=by, z=bz), 1, "cyz", b_sem, finish(sum_b))

        def block_of(rank):
            r = rank % 16
            return full_v.at[rank // 16, r // 4, (r // 2) % 2, r % 2]

        spot = (place.m, place.z, place.y, place.c)
        all_v = Everyone(place, block_of, lambda step: land_v.at[step - 1], v_sem)
        all_n = Everyone(place, lambda rank: norms.at[spot], lambda step: norms.at[spot], n_sem)

        def background(number):
            tree_e.event(number)

        background(0)
        fill.wait()
        for k in early:
            loads[k].wait()

    boxt[...] = box_ref[...].T
    gbox[...] = jnp.zeros_like(gbox)

    def prepare(page, carry):
        rows = aligned(page, PAGE)
        kftok[rows, :] = kft_ref[:, rows].T
        dctxt[:, rows] = dctx_ref[rows, :].T
        xt[:, rows] = x_ref[rows, :].T
        if plan is not None:
            pl.when(page == pages - 1)(lambda: background(1))
        return carry

    lax.fori_loop(0, pages, prepare, 0)
    if plan is not None:
        for k in range(12):
            if k not in early:
                loads[k].wait()

    def attend(step, carry):
        page, pair = step // (heads // 2), step % (heads // 2)
        rows = aligned(page, PAGE)
        own, partner = turn_factors(trig_ref[:, rows])
        pair_lanes = aligned(pair, 2 * HD)
        query_pair = qtok_ref[rows, pair_lanes]
        dctx_pair = dctx_ref[rows, pair_lanes]
        halves = []
        boxes = []
        blank = jnp.zeros((HD, PAGE), BF16)
        for side in range(2):
            head = pair * 2 + side
            lanes = aligned(head, 2 * HD)
            key_value = kvtok_ref[rows, lanes]
            left = jnp.concatenate([kftok[rows, :], key_value], axis=1)
            score = dot(left, jnp.concatenate([qa_ref[head, :, rows], blank], axis=0))
            prob = jnp.exp(score - log_ref[head, :, rows])
            prob_low = prob.astype(BF16)
            head_rows = pl.ds(pl.multiple_of(head * HD, HD), HD)
            dctx_head = dctxt[head_rows, rows]
            grad_prob = dot(
                key_value, jnp.concatenate([blank, dctx_head], axis=0)
            )
            inner = col_sum(dctx_head.astype(F32) * ctxt_ref[head_rows, rows].astype(F32))
            grad_score = (prob * (grad_prob - inner)).astype(BF16)
            if side == 0:
                both = jnp.concatenate([query_pair[:, 0:HD], dctx_pair[:, 0:HD]], axis=1)
            else:
                both = jnp.concatenate([query_pair[:, HD:], dctx_pair[:, HD:]], axis=1)
            from_score = dot(grad_score, both)
            from_prob = dot(prob_low, both)
            grad_kv = jnp.where(lower, from_score, from_prob).astype(BF16)
            dtok[rows, pl.ds(pl.multiple_of(cols + head * 2 * HD, 2 * HD), 2 * HD)] = grad_kv
            keys = jnp.concatenate([kft_ref[:, rows], kt_ref[head_rows, rows]], axis=0)
            grad_query = dot(keys, grad_score) * HD ** (-0.5)
            feat = grad_query[0:PE]
            proj = (feat * own - swap_blocks(feat) * partner).astype(BF16)
            halves.append(grad_query[PE:] + dot(boxt[head_rows, :], proj))
            boxes.append(dot(proj, query_pair))
        gbox[:, pair_lanes] += jnp.where(lower, boxes[0], boxes[1])
        dtok[rows, pair_lanes] = jnp.concatenate(halves, axis=0).astype(BF16).T
        return carry

    def spread(page):
        rows = aligned(page, PAGE)
        return sum(
            dot(dtok[rows, chunk * UNIT : (chunk + 1) * UNIT], w_ref[chunk], NT) for chunk in range(3)
        )

    if plan is None:
        lax.fori_loop(0, pages * (heads // 2), attend, 0)
        gbox_ref[...] = gbox[...] * HD**0.5

        def spread_page(page, carry):
            inp_ref[aligned(page, PAGE), :] = spread(page)
            return carry

        lax.fori_loop(0, pages, spread_page, 0)

        def gather(step, carry):
            lanes = aligned(step, UNIT)
            gw_ref[step] = dot(xt[...], dtok[:, lanes]).astype(BF16)
            qvsum_ref[0:1, lanes] = col_sum(dtok[:, lanes].astype(F32))
            return carry

        lax.fori_loop(0, 3, gather, 0)
        return

    def swap(index):
        rows = aligned(index, piece)
        return remote(
            inp_ref.at[rows, :], came.at[rows, :], i_sem.at[0, index], i_sem.at[1, index], place.peer["x"]
        )

    def attend_and_send(step, carry):
        attend(step, carry)
        page = step // (heads // 2)

        @pl.when(step % (heads // 2) == heads // 2 - 1)
        def _():
            value = spread(page)
            for half in range(2):
                index = 2 * page + half
                rows = aligned(index, piece)
                own = index // pages == m
                spot = aligned(index % pages, piece)
                extra = jnp.where(own, dh1_ref[spot, :].astype(F32), 0.0)
                inp_ref[rows, :] = (value[half * piece : (half + 1) * piece] + extra).astype(BF16)
                start_rows(
                    inp_ref.at[rows, :],
                    came.at[rows, :],
                    piece,
                    i_sem.at[0, index],
                    i_sem.at[1, index],
                    place.peer["x"],
                )

        pl.when(step % 3 != 2)(lambda: background(2 + 2 * (step // 3) + step % 3))
        return carry

    lax.fori_loop(0, pages * (heads // 2), attend_and_send, 0)
    put_natural(full_b, 0, 0, gbox[...] * HD**0.5)

    def gather(step, carry):
        grad = dot(xt[...], dtok[:, aligned(step, UNIT)]).astype(BF16)
        put_natural(full_a, step, 0, grad)
        tree_a.event(step)
        tree_b.event(step)
        background(8 + step)
        return carry

    lax.fori_loop(0, 3, gather, 0)

    sums = jnp.concatenate(
        [
            col_sum(dtok[:, chunk * UNIT : (chunk + 1) * UNIT].astype(F32)) for chunk in range(3)
        ],
        axis=1,
    )
    values = exact_dot(jnp.broadcast_to(sums[:, cols:], (8, 2 * cols)), pair_place(cols), NT)
    pair = jnp.concatenate([sums[:, 0:cols], values[0:1]], axis=0)
    blank = jnp.zeros_like(pair)
    pair = jnp.where(
        m == 0, jnp.concatenate([pair, blank], axis=1), jnp.concatenate([blank, pair], axis=1)
    )
    table = jnp.concatenate([vsum_ref[0:6, :], pair, vsum_ref[8:, :]], axis=0)
    mp_count, dp_count = plan
    width = table.shape[1]
    each = width // (mp_count * dp_count)
    wide_lane = lax.broadcasted_iota(jnp.int32, (VROWS, width), 1)
    for side in range(mp_count):
        parts = []
        for r in range(dp_count):
            first = (r * mp_count + side) * each
            parts.append(jnp.where((wide_lane >= first) & (wide_lane < first + each), table, 0.0))
        block = exact_dot(jnp.concatenate(parts, axis=0), pick_ref[...], NT)
        full_v[side] = block.reshape(full_v.shape[1:])
    all_v.start()

    def tail(number, carry):
        tree_a.event(number)
        tree_b.event(number)
        return carry

    lax.fori_loop(3, tree_a.events, tail, 0)
    tree_e.rest()
    all_v.wait()
    total_v = full_v[spot] + jnp.sum(land_v[...], axis=0)
    sum_v[0] = total_v * inv_tokens

    square = sum(jnp.sum(out[...] * out[...]) for out in (sum_e, sumf_ref, sum_a, sum_b, sum_v))
    norms[spot] = jnp.full((8, 128), square, F32)
    all_n.start()

    def final(number, carry):
        rows = aligned(number, piece)
        swap(number).wait()
        inp_ref[rows, :] = (inp_ref[rows, :].astype(F32) + came[rows, :].astype(F32)).astype(BF16)
        return carry

    lax.fori_loop(0, pieces, final, 0)
    all_n.wait()
    every = norms[...].reshape(-1, 8, 128)
    norm_ref[...] = jnp.sqrt(sum(every[k] for k in range(every.shape[0])))
    for tree in (tree_e, tree_a, tree_b):
        tree.drain()


def attend_backward(x, weight, box, kept, dctx, plan, inv_tokens, more=()):
    tokens, width = x.shape
    cols = weight.shape[-1]
    heads = cols // HD
    vmem = pl.BlockSpec(memory_space=pltpu.VMEM)
    scratch = [
        pltpu.VMEM((tokens, PE), BF16),
        pltpu.VMEM((cols, tokens), BF16),
        pltpu.VMEM((cols, PE), BF16),
        pltpu.VMEM((tokens, 3 * cols), BF16),
        pltpu.VMEM((width, tokens), BF16),
        pltpu.VMEM((PE, cols), F32),
    ]
    in_specs = [vmem] * 12
    if plan is None:
        shapes = [
            ((tokens, width), F32),
            ((3, width, cols), BF16),
            ((PE, cols), F32),
            ((8, 3 * cols), F32),
        ]
        extra = {}
    else:
        free = pl.BlockSpec(memory_space=pl.ANY)
        in_specs = [free] * 12 + [vmem] * 4 + [free]
        rows = width // 16
        unit = (rows, UNIT)
        tile = (PE // 16, cols)
        small = (VROWS, 128)
        shapes = [
            ((tokens, width), BF16),
            ((5, *unit), F32),
            ((3, *unit), F32),
            ((1, *tile), F32),
            ((1, *small), F32),
            ((8, 128), F32),
        ]
        scratch += [
            pltpu.VMEM((tokens, width), BF16),
            pltpu.VMEM((5, 2, 4, 2, *unit), BF16),
            pltpu.VMEM((3, 2, 1, 4, 2, *unit), BF16),
            pltpu.VMEM((1, 2, 1, 4, 2, *tile), F32),
            pltpu.VMEM((2, 4, 2, 2, *small), F32),
            pltpu.VMEM((31, *small), F32),
            pltpu.VMEM((2, 4, 2, 2, 8, 128), F32),
            pltpu.VMEM((5, 2, 4, 2, *unit), BF16),
            pltpu.VMEM((5, 2, 4, *unit), BF16),
            pltpu.VMEM((5, 3, 2, *unit), BF16),
            pltpu.VMEM((5, *unit), BF16),
            pltpu.VMEM((3, 4, 2, *unit), BF16),
            pltpu.VMEM((3, 4, *unit), BF16),
            pltpu.VMEM((3, 3, *unit), BF16),
            pltpu.VMEM((1, 4, 2, *tile), F32),
            pltpu.VMEM((1, 4, *tile), F32),
            pltpu.VMEM((1, 3, *tile), F32),
            pltpu.SemaphoreType.DMA((2, 5, SLOTS)),
            pltpu.SemaphoreType.DMA((2, 3, SLOTS)),
            pltpu.SemaphoreType.DMA((2, 1, SLOTS)),
            pltpu.SemaphoreType.DMA((2, 31)),
            pltpu.SemaphoreType.DMA((2, 31)),
            pltpu.SemaphoreType.DMA((2, 2 * (tokens // PAGE))),
            pltpu.SemaphoreType.DMA((2,)),
        ]
        scratch += [pltpu.VMEM(array.shape, array.dtype) for array in (x, weight, box, *kept, dctx)]
        scratch.append(pltpu.SemaphoreType.DMA((12,)))
        extra = dict(collective_id=2, has_side_effects=True)
    return pl.pallas_call(
        functools.partial(attend_back_kernel, heads, plan, inv_tokens),
        out_shape=[jax.ShapeDtypeStruct(s, d) for s, d in shapes],
        in_specs=in_specs,
        out_specs=[vmem] * len(shapes),
        scratch_shapes=scratch,
        compiler_params=pltpu.CompilerParams(vmem_limit_bytes=VMEM_LIMIT, **extra),
        cost_estimate=pl.CostEstimate(flops=4 * 10**10, bytes_accessed=10**8, transcendentals=10**7),
        name="attend_backward",
    )(x, weight, box, *kept, dctx, *more)


def adam_step(master, first, second, gradient, rate, decay):
    new_first = BETA_ONE * first + (1.0 - BETA_ONE) * gradient
    new_second = BETA_TWO * second + (1.0 - BETA_TWO) * gradient * gradient
    first_hat = new_first / (1.0 - BETA_ONE**STEP)
    second_hat = new_second / (1.0 - BETA_TWO**STEP)
    new_master = master - rate * (first_hat / (jnp.sqrt(second_hat) + ADAM_EPS) + decay * master)
    return (new_first, new_second, new_master)


def adam_kernel(heads, norm_ref, *refs):
    sum_e, sum_f, sum_a, sum_b, sum_v, *refs = refs
    states, outs = refs[:18], refs[18:]
    outs[-1][...] = norm_ref[0:1, 0:1]
    clip = CLIP_LIMIT / jnp.maximum(norm_ref[0:1, 0:1], CLIP_LIMIT)

    def update(first, out, gradient, at, rate, decay):
        news = adam_step(*(ref[at] for ref in states[first : first + 3]), gradient * clip, rate, decay)
        for ref, new in zip(outs[out : out + 3], news):
            ref[at] = new
        if decay:
            outs[out + 3][at] = news[2].astype(BF16)

    def heads_of(kind):
        half = heads // 2
        return jnp.concatenate(
            [
                sum_a[1 + head // half, :, (2 * (head % half) + kind) * HD : (2 * (head % half) + kind + 1) * HD]
                for head in range(heads)
            ],
            axis=1,
        )

    for index, gradient in enumerate((sum_a[0], heads_of(0), heads_of(1))):
        update(0, 0, gradient, index, RATE_MATRIX, WEIGHT_DECAY)
    update(3, 4, sum_b[0], ALL, RATE_MATRIX, WEIGHT_DECAY)
    update(6, 8, sum_e[0], ALL, RATE_MATRIX, WEIGHT_DECAY)
    for chunk in range(4):
        lanes = (ALL, slice(chunk * UNIT, (chunk + 1) * UNIT))
        update(9, 12, sum_e[1 + chunk], lanes, RATE_MATRIX, WEIGHT_DECAY)
        update(12, 16, sum_f[chunk], lanes, RATE_MATRIX, WEIGHT_DECAY)
    rows, each = states[15].shape
    update(15, 20, sum_v[0, 0:rows, 0:each], ALL, RATE_VECTOR, 0.0)


def adam_all(norm, sums, states):
    shapes = []
    for first in range(0, 18, 3):
        shapes += [(states[first].shape, F32)] * 3
        if first < 15:
            shapes.append((states[first].shape, BF16))
    vmem = pl.BlockSpec(memory_space=pltpu.VMEM)
    shapes.append(((1, 1), F32))
    return pl.pallas_call(
        functools.partial(adam_kernel, states[0].shape[2] // HD),
        out_shape=[jax.ShapeDtypeStruct(s, d) for s, d in shapes],
        in_specs=[vmem] * (6 + len(states)),
        out_specs=[vmem] * len(shapes),
        compiler_params=pltpu.CompilerParams(vmem_limit_bytes=VMEM_LIMIT),
        name="adam_all",
    )(norm, *sums, *states)


def pack_qkv(shard):
    rows, cols = shard.shape[1:]
    heads = cols // HD
    pairs = jnp.stack([shard[1].reshape(rows, heads, HD), shard[2].reshape(rows, heads, HD)], axis=2)
    pairs = pairs.reshape(rows, 2, cols)
    return jnp.stack([shard[0], pairs[:, 0], pairs[:, 1]])


def unpack_qkv(packed):
    rows, cols = packed.shape[1:]
    pairs = jnp.concatenate([packed[1], packed[2]], axis=1).reshape(rows, cols // HD, 2, HD)
    return jnp.stack(
        [packed[0], pairs[:, :, 0].reshape(rows, cols), pairs[:, :, 1].reshape(rows, cols)]
    )


def to_chunks(shard):
    rows = shard.shape[0]
    return shard.reshape(rows, -1, UNIT).transpose(1, 0, 2)


def from_chunks(chunks):
    return chunks.transpose(1, 0, 2).reshape(chunks.shape[1], -1)


def on_device(
    layer_input,
    page_boxes,
    output_grad,
    attn_proj,
    attn_first,
    attn_second,
    box_proj,
    box_first,
    box_second,
    merge_proj,
    merge_first,
    merge_second,
    expand_proj,
    expand_first,
    expand_second,
    shrink_proj,
    shrink_first,
    shrink_second,
    vectors,
    vector_first,
    vector_second,
):
    mp_count = lax.axis_size("mp")
    dp_count = lax.axis_size("dp")
    mp_index = lax.axis_index("mp")
    tokens, width = layer_input.shape
    cols = attn_proj.shape[2]
    heads = cols // HD
    own_tokens = tokens // mp_count
    inv_tokens = 1.0 / (tokens * dp_count)

    corners = page_boxes.T
    omega = (10000.0 ** (-np.arange(FREQS, dtype=np.float64) / FREQS)).astype(np.float32)[:, None]
    omega = jnp.asarray(omega)
    plan = (mp_count, dp_count) if dp_count == 16 and mp_count == 2 else None
    if plan is not None:
        each = vectors.shape[1]
        pick = np.zeros((128, width), np.float32)
        pick[np.arange(width) % each, np.arange(width)] = 1.0
        pick = jnp.asarray(pick)
        *kept, w_qkv, w_box, layer_out, dctx, dh1, g_expand, vec_sum, sum_f = layer_forward(
            layer_input,
            output_grad,
            corners,
            omega,
            pick,
            (attn_proj, box_proj, vectors, merge_proj.T, expand_proj, shrink_proj.T),
            plan,
            inv_tokens,
        )
        input_grad, sum_e, sum_a, sum_b, sum_v, norm = attend_backward(
            layer_input,
            w_qkv,
            w_box,
            kept,
            dctx,
            plan,
            inv_tokens,
            (dh1, vec_sum, sum_f, pick, g_expand),
        )
        merge = [merge_proj.T, merge_first.T, merge_second.T]
        shrink = [shrink_proj.T, shrink_first.T, shrink_second.T]
        *results, norm = adam_all(
            norm,
            (sum_e, sum_f, sum_a, sum_b, sum_v),
            [attn_proj, attn_first, attn_second, box_proj, box_first, box_second, *merge]
            + [expand_proj, expand_first, expand_second, *shrink, vectors, vector_first, vector_second],
        )
        turned = (8, 9, 10, 11, 16, 17, 18, 19)
        results = [out.T if k in turned else out for k, out in enumerate(results)]
        return (layer_out, input_grad, norm.reshape(()), *results)
    shard_qkv = pack_qkv(attn_proj).astype(BF16)
    shard_e = jnp.concatenate([merge_proj.T[None], to_chunks(expand_proj)]).astype(BF16)
    shard_f = to_chunks(shrink_proj.T).astype(BF16)
    w_qkv = lax.all_gather(shard_qkv, "dp", axis=1, tiled=True)
    w_box = lax.all_gather(box_proj.astype(BF16), "dp", axis=0, tiled=True)
    w_expand = lax.all_gather(lax.all_gather(shard_e, "dp", axis=1, tiled=True), "mp", axis=1)
    w_shrink = lax.all_gather(lax.all_gather(shard_f, "dp", axis=1, tiled=True), "mp", axis=1)
    vecs = lax.all_gather(vectors, ("dp", "mp"), axis=1, tiled=True)
    vecs = jnp.pad(vecs, ((0, VROWS - vecs.shape[0]), (0, 0)))
    *kept, context = attend_forward(layer_input, corners, omega, w_qkv, w_box, vecs)
    context = lax.all_to_all(
        context.reshape(mp_count, own_tokens, cols), "mp", split_axis=0, concat_axis=0
    )

    def own_rows(array):
        return lax.dynamic_slice_in_dim(array, mp_index * own_tokens, own_tokens)

    layer_out, dctx, dh1, g_expand, g_shrink, vec_sum = feed_both(
        own_rows(layer_input), own_rows(output_grad), context, w_expand, w_shrink, vecs
    )
    g_feed = jnp.concatenate([g_expand, g_shrink])
    layer_out = lax.all_gather(layer_out, "mp", axis=0, tiled=True)
    dctx = lax.all_to_all(dctx, "mp", split_axis=0, concat_axis=0).reshape(tokens, cols)
    part, g_qkv, g_box, qkv_sum = attend_backward(
        layer_input, w_qkv, w_box, kept, dctx, None, inv_tokens
    )
    own_part = lax.psum_scatter(part.astype(BF16), "mp", scatter_dimension=0, tiled=True)
    own_grad = (own_part.astype(F32) + dh1).astype(BF16)
    input_grad = lax.all_gather(own_grad, "mp", axis=0, tiled=True)
    shard_attn = unpack_qkv(
        lax.psum_scatter(g_qkv, "dp", scatter_dimension=1, tiled=True).astype(F32) * inv_tokens
    )
    shard_box = lax.psum_scatter(g_box, "dp", scatter_dimension=0, tiled=True) * inv_tokens
    sum_feed = lax.psum_scatter(g_feed, "dp", scatter_dimension=2, tiled=True)
    sum_feed = lax.psum_scatter(sum_feed, "mp", scatter_dimension=1, tiled=True)[:, 0]
    sum_feed = sum_feed.astype(F32) * inv_tokens
    sum_expand, sum_shrink = sum_feed[0:5], sum_feed[5:]

    def placed(row):
        return lax.dynamic_update_slice_in_dim(
            jnp.zeros((width,), F32), row, mp_index * cols, 0
        )[None, :]

    value_sum = qkv_sum[0, cols:].reshape(heads, 2, HD)[:, 1].reshape(cols)
    vector_grad = jnp.concatenate(
        [vec_sum[0:6], placed(qkv_sum[0, 0:cols]), placed(value_sum), vec_sum[8:12]]
    )
    vector_shard = (
        lax.psum_scatter(vector_grad, ("dp", "mp"), scatter_dimension=1, tiled=True) * inv_tokens
    )
    square = sum(
        jnp.sum(shard * shard)
        for shard in (shard_attn, shard_box, sum_expand, sum_shrink, vector_shard)
    )
    grad_norm = jnp.sqrt(lax.psum(square, ("dp", "mp")))
    shard_merge = sum_expand[0].T
    shard_expand = from_chunks(sum_expand[1:])
    shard_shrink = from_chunks(sum_shrink).T
    clip_scale = CLIP_LIMIT / jnp.maximum(grad_norm, CLIP_LIMIT)
    results = [layer_out, input_grad, grad_norm]
    for master, first, second, shard in (
        (attn_proj, attn_first, attn_second, shard_attn),
        (box_proj, box_first, box_second, shard_box),
        (merge_proj, merge_first, merge_second, shard_merge),
        (expand_proj, expand_first, expand_second, shard_expand),
        (shrink_proj, shrink_first, shrink_second, shard_shrink),
    ):
        new_first, new_second, new_master = adam_step(
            master, first, second, shard * clip_scale, RATE_MATRIX, WEIGHT_DECAY
        )
        results += [new_first, new_second, new_master, new_master.astype(BF16)]
    results += adam_step(
        vectors, vector_first, vector_second, vector_shard * clip_scale, RATE_VECTOR, 0.0
    )
    return tuple(results)


def solution(mesh):
    rows = P("dp", None)
    attn = P(None, "dp", "mp")
    tall = P("dp", "mp")
    wide = P("mp", "dp")
    vector = P(None, ("dp", "mp"))
    in_specs = (rows,) * 3 + (attn,) * 3 + (tall,) * 3 + (wide,) * 3 + (tall,) * 3 + (wide,) * 3
    in_specs += (vector,) * 3
    out_specs = (rows, rows, P()) + (attn,) * 4 + (tall,) * 4 + (wide,) * 4 + (tall,) * 4
    out_specs += (wide,) * 4 + (vector,) * 3
    return jax.shard_map(
        on_device, mesh=mesh, in_specs=in_specs, out_specs=out_specs, check_vma=False
    )
```

profile of v0, /device:TPU:0, one launch (start us, length us, event | category | flops | bytes accessed | tf_op | source)
XLA Modules:
  0.0 248.3 jit_solution(2152821399055140430)
XLA Ops:
  0.7 153.5 %layer_forward.1 = (bf16[6,192,1536]{2,1,0:T(8,128)(2,1)}, bf16[1536,384]{1,0:T(8,128)(2,1)}, bf16[1536,768]{1,0:T(8,128)(2,1)}, bf16[384,1536]{1,0:T(8,128)(2,1...) custom-call(bf16[1536,768]{1,0:T(8,128)(2,1)} %refs_0_.3, ...), custom_call_target="tpu_custom_call" | custom-call | tf_op jit(solution)/shard_map/layer_forward/pallas_call | solution.py:1001
  154.2 85.9 %attend_backward.1 = (bf16[1536,768]{1,0:T(8,128)(2,1)}, f32[5,48,384]{2,1,0:T(8,128)}, f32[3,48,384]{2,1,0:T(8,128)}, f32[1,8,384]{2,1,0:T(8,128)}, f32[1,16,128]{2,1,0:T(8,128)}, /*index=5*/f32[8,128]{1,0:T(8,128)}) custom-call(bf16[1536,768]{1,0:T(8,128)(2,1)} %refs_0_.3, bf16[3,768,384]{2,1,0:T(8,128)(2,1)} %get-tuple-element.73.refs_1_, ...), custom_call_target="tpu_custom_call" | custom-call | flops 40000000000 | bytes 100000000 | tf_op jit(solution)/shard_map/attend_backward/pallas_call | solution.py:1349
  240.1 0.0 copy-start
  240.1 4.3 %adam_all.1 = (f32[3,48,384]{2,1,0:T(8,128)}, f32[3,48,384]{2,1,0:T(8,128)}, f32[3,48,384]{2,1,0:T(8,128)}, bf16[3,48,384]{2,1,0:T(8,128)(2,1)}, f32[8,384]{1,0:...) custom-call(f32[8,128]{1,0:T(8,128)} %get-tuple-element.89.norm_ref,, ...), custom_call_target="tpu_custom_call" | custom-call | tf_op jit(solution)/shard_map/adam_all/pallas_call | solution.py:1413
  244.4 0.0 copy-done
  244.4 0.0 copy-start.1
  244.4 1.4 copy.51
  245.8 1.1 copy-done.1
  246.9 1.4 copy.52
Async XLA Ops:
  240.1 4.3 %copy-start = (bf16[1536,768]{1,0:T(8,128)(2,1)S(1)}, bf16[1536,768]{1,0:T(8,128)(2,1)}, u32[]{:S(2)}) copy-start(bf16[1536,768]{1,0:T(8,128)(2,1)} %get-tuple-element.144) | copy-start | bytes 7077892
  244.4 2.5 %copy-start.1 = (bf16[1536,768]{1,0:T(8,128)(2,1)S(1)}, bf16[1536,768]{1,0:T(8,128)(2,1)}, u32[]{:S(2)}) copy-start(bf16[1536,768]{1,0:T(8,128)(2,1)} %get-tuple-element.145) | copy-start | bytes 7077892
where the time goes:
time: 249 us; the launch traced here: 248 us
  Pallas kernels  244 us (98%)
  local copies, waits for them, and re-layouts  3.92 us (2%)
    pallas_call x1, Pallas kernels, layer_forward(): pl.pallas_call(functools.partial(layer_kernel, heads, plan, inv_tokens, n...  154 us
    pallas_call x1, Pallas kernels, attend_backward(): pl.pallas_call(functools.partial(attend_back_kernel, heads, plan, inv_tok...  85.9 us

commit v1 on v0

--- a/solution.py
+++ b/solution.py
@@ -915,11 +915,11 @@
             pl.when(step != 2)(lambda: back_f.event(step - step // 3))
 
         def shrank(number):
-            for spot, event in ((1, 3), (4, 4), (8, 5), (11, 6)):
+            for spot, event in ((2, 3), (6, 4), (11, 5)):
                 pl.when(number == spot)(lambda event=event: back_f.event(event))
 
         def expands(step):
-            pl.when(step != 1)(lambda: back_f.event(7 + (step + 1) // 2))
+            back_f.event(6 + step)
 
         load_x.wait()
         load_og.wait()

time: 249 us -> 249 us (level)
  no operation moved by 1% of the time
where the time goes in v1:
time: 249 us; the launch traced here: 248 us
  Pallas kernels  244 us (98%)
  local copies, waits for them, and re-layouts  3.92 us (2%)
    pallas_call x1, Pallas kernels, layer_forward(): pl.pallas_call(functools.partial(layer_kernel, heads, plan, inv_tokens, n...  153 us
    pallas_call x1, Pallas kernels, attend_backward(): pl.pallas_call(functools.partial(attend_back_kernel, heads, plan, inv_tok...  86.3 us

profile of v1, /device:TPU:0, one launch (start us, length us, event | category | flops | bytes accessed | tf_op | source)
XLA Modules:
  0.0 248.3 jit_solution(16200226836361562247)
XLA Ops:
  0.7 153.1 %layer_forward.1 = (bf16[6,192,1536]{2,1,0:T(8,128)(2,1)}, bf16[1536,384]{1,0:T(8,128)(2,1)}, bf16[1536,768]{1,0:T(8,128)(2,1)}, bf16[384,1536]{1,0:T(8,128)(2,1...) custom-call(bf16[1536,768]{1,0:T(8,128)(2,1)} %refs_0_.3, ...), custom_call_target="tpu_custom_call" | custom-call | tf_op jit(solution)/shard_map/layer_forward/pallas_call | solution.py:1001
  153.8 86.3 %attend_backward.1 = (bf16[1536,768]{1,0:T(8,128)(2,1)}, f32[5,48,384]{2,1,0:T(8,128)}, f32[3,48,384]{2,1,0:T(8,128)}, f32[1,8,384]{2,1,0:T(8,128)}, f32[1,16,128]{2,1,0:T(8,128)}, /*index=5*/f32[8,128]{1,0:T(8,128)}) custom-call(bf16[1536,768]{1,0:T(8,128)(2,1)} %refs_0_.3, bf16[3,768,384]{2,1,0:T(8,128)(2,1)} %get-tuple-element.73.refs_1_, ...), custom_call_target="tpu_custom_call" | custom-call | flops 40000000000 | bytes 100000000 | tf_op jit(solution)/shard_map/attend_backward/pallas_call | solution.py:1349
  240.1 0.0 copy-start
  240.1 4.3 %adam_all.1 = (f32[3,48,384]{2,1,0:T(8,128)}, f32[3,48,384]{2,1,0:T(8,128)}, f32[3,48,384]{2,1,0:T(8,128)}, bf16[3,48,384]{2,1,0:T(8,128)(2,1)}, f32[8,384]{1,0:...) custom-call(f32[8,128]{1,0:T(8,128)} %get-tuple-element.89.norm_ref,, ...), custom_call_target="tpu_custom_call" | custom-call | tf_op jit(solution)/shard_map/adam_all/pallas_call | solution.py:1413
  244.4 0.0 copy-done
  244.4 0.0 copy-start.1
  244.4 1.4 copy.51
  245.8 1.1 copy-done.1
  246.9 1.4 copy.52
Async XLA Ops:
  240.1 4.3 %copy-start = (bf16[1536,768]{1,0:T(8,128)(2,1)S(1)}, bf16[1536,768]{1,0:T(8,128)(2,1)}, u32[]{:S(2)}) copy-start(bf16[1536,768]{1,0:T(8,128)(2,1)} %get-tuple-element.144) | copy-start | bytes 7077892
  244.4 2.5 %copy-start.1 = (bf16[1536,768]{1,0:T(8,128)(2,1)S(1)}, bf16[1536,768]{1,0:T(8,128)(2,1)}, u32[]{:S(2)}) copy-start(bf16[1536,768]{1,0:T(8,128)(2,1)} %get-tuple-element.145) | copy-start | bytes 7077892
